TPU v7x, 256 devices: a whole 4x4x8 slice. The times are simulated.
256 devices in a mesh: row: 8 (over x, core), col: 32 (over z, y).
Axes of the slice: x: 4, y: 4, z: 8, core: 2. Of those that a mesh axis runs over, the one named last changes fastest.
Arguments:
- base_mttkrp: float32 [512, 128], P('row'), may hold values from -6 to 6
- operator_b: bfloat16 [512, 8192, 128], P('row', 'col'), may hold values from -6 to 6
- operator_c: bfloat16 [512, 8192, 128], P('row', 'col'), may hold values from -6 to 6
- delta_b: bfloat16 [8192, 128], P('col', 'row'), may hold values from -0.0625 to 0.0625
- delta_c: bfloat16 [8192, 128], P('col', 'row'), may hold values from -0.0625 to 0.0625
- factor_b: float32 [8192, 128], P('col', 'row'), may hold values from 0 to 2
- factor_c: float32 [8192, 128], P('col', 'row'), may hold values from 0 to 2
Outputs:
- factor_a: float32 [512, 128], P('row')
- gram_next: float32 [128, 128], replicated
All inputs are finite; a program needn't handle non-finite values.
Results may differ from a plain program's by a relative error of at most 0.0003.
Values may be sent and summed in bfloat16 or wider, within the bound.
A program may use at most 64 MiB of HBM per device.

v0:
```python
import jax
import jax.numpy as jnp
from jax import lax
from jax.sharding import PartitionSpec as P

J = 8192
K = 8192


def solve_rows(mttkrp, lower):
    inner = jax.scipy.linalg.solve_triangular(lower, mttkrp.T, lower=True)
    return jax.scipy.linalg.solve_triangular(lower, inner, lower=True, trans=1).T


def gram_of(matrix):
    return jnp.dot(matrix.T, matrix, precision=lax.Precision.HIGHEST)


def shards(base_mttkrp, operator_b, operator_c, delta_b, delta_c, factor_b, factor_c):
    full_db, full_dc = (
        lax.all_gather(delta_b, "row", axis=1, tiled=True),
        lax.all_gather(delta_c, "row", axis=1, tiled=True),
    )
    full_b, full_c = (
        lax.all_gather(factor_b, "row", axis=1, tiled=True),
        lax.all_gather(factor_c, "row", axis=1, tiled=True),
    )
    contraction = jnp.einsum("ijr,jr->ir", operator_b, full_db, preferred_element_type=jnp.float32)
    contraction = contraction + jnp.einsum(
        "ijr,jr->ir", operator_c, full_dc, preferred_element_type=jnp.float32
    )
    summed = None
    gram_b, gram_c = lax.psum((gram_of(full_b), gram_of(full_c)), "col")
    hadamard = gram_b / J * (gram_c / K)
    lower = jnp.linalg.cholesky(hadamard)
    total_rows = base_mttkrp.shape[0] * lax.axis_size("row")
    summed = lax.psum(contraction, "col")
    factor_a = solve_rows(base_mttkrp + summed, lower)
    gram_a = lax.psum(gram_of(factor_a), "row")
    gram_next = gram_a / total_rows * (gram_c / K)
    return (factor_a, gram_next)


def solution(mesh):
    return jax.shard_map(
        shards,
        mesh=mesh,
        in_specs=(
            P("row", None),
            P("row", "col", None),
            P("row", "col", None),
            P("col", "row"),
            P("col", "row"),
            P("col", "row"),
            P("col", "row"),
        ),
        out_specs=(P("row", None), P()),
        check_vma=False,
    )
```

profile of v0, /device:TPU:1, one launch (start us, length us, event | category | flops | bytes accessed | tf_op | source)
XLA Modules:
  0.0 304.4 jit_solution(7137814588511449537)
XLA Ops:
  7.2 0.0 all-reduce.6.cloned.1.call-start
  7.2 16.0 %all_gather.12 = f32[256,128]{0,1:T(8,128)S(1)} all-gather(f32[256,16]{0,1:T(8,128)} %param.12), channel_id=1, replica_groups=mesh['row'=8,'col'=32] {'row'}, dimensions={1}, use_global_device_ids=true | all-gather | bytes 147456 | tf_op jit(solution)/shard_map/all_gather | solution.py:25
  23.2 0.9 fusion.7
  24.2 12.9 %all_gather.13 = f32[256,128]{0,1:T(8,128)S(1)} all-gather(f32[256,16]{0,1:T(8,128)} %param.13), channel_id=1, replica_groups=mesh['row'=8,'col'=32] {'row'}, dimensions={1}, use_global_device_ids=true | all-gather | bytes 147456 | tf_op jit(solution)/shard_map/all_gather | solution.py:26
  37.1 0.9 fusion.8
  38.0 0.0 all-reduce.6.cloned.1.call-update
  38.0 0.0 all-reduce.4.cloned.1.call-start
  38.1 12.9 %all_gather.14 = bf16[256,128]{0,1:T(8,128)(2,1)S(1)} all-gather(bf16[256,16]{0,1:T(8,128)(2,1)} %param.10), channel_id=1, replica_groups=mesh['row'=8,'col'=32] {'row'}, dimensions={1}, use_global_device_ids=true | all-gather | bytes 73728 | tf_op jit(solution)/shard_map/all_gather | solution.py:21
  51.0 0.1 copy.31
  51.1 13.0 %all_gather.15 = bf16[256,128]{0,1:T(8,128)(2,1)S(1)} all-gather(bf16[256,16]{0,1:T(8,128)(2,1)} %param.11), channel_id=1, replica_groups=mesh['row'=8,'col'=32] {'row'}, dimensions={1}, use_global_device_ids=true | all-gather | bytes 73728 | tf_op jit(solution)/shard_map/all_gather | solution.py:22
  64.1 0.1 copy.32
  64.2 0.0 copy-start.1
  64.2 6.1 %multiply_reduce_fusion = (f32[128,64]{0,1:T(8,128)S(1)}, f32[128,64]{0,1:T(8,128)S(1)}) fusion(f32[128,256]{0,1:T(8,128)S(1)} %copy.32, bf16[64,256,128]{2,1,0:T(8,128)(2,1)} %param.9, bf16[64,256,128]{2,1,0:T(8,128)(2,1)} %param.8, f32[128,256]{0,1:T(8,128)S(1)} %copy.31), kind=kLoop, calls=%fused_computation | loop fusion | flops 12566528 | bytes 8716288 | tf_op jit(solution)/shard_map/ijr,jr->ir/dot_general | solution.py:29
  70.4 117.3 %psum.30 = f32[64,128]{1,0:T(8,128)S(1)} all-reduce(f32[64,128]{1,0:T(8,128)S(1)} %add_bitcast_fusion), channel_id=1, replica_groups=mesh['row'=8,'col'=32] {'col'}, use_global_device_ids=true, to_apply=%region_4.5 | all-reduce | flops 8192 | bytes 65536 | tf_op jit(solution)/shard_map/psum | solution.py:37
  187.7 0.0 all-reduce.6.cloned.1.call-done
  187.7 0.9 multiply_multiply_fusion.1
  188.6 0.1 copy.11
  188.7 11.7 %cholesky.16 = f32[128,128]{1,0:T(8,128)S(1)} custom-call(f32[128,128]{1,0:T(8,128)S(1)} %fusion.5), custom_call_target="Cholesky" | custom-call | tf_op jit(solution)/shard_map/jit(cholesky)/cholesky | solution.py:35
  200.5 0.6 compare_reduce_fusion
  201.1 0.7 fusion
  201.8 9.8 %custom-call.10 = f32[1,128,128]{1,2,0:T(8,128)S(1)} custom-call(f32[1,128,128]{2,1,0:T(8,128)S(1)} %fusion), custom_call_target="InvertDiagBlocksLowerTriangular" | custom-call | tf_op jit(solution)/shard_map/jit(_solve_triangular)/triangular_solve | solution.py:12
  211.6 0.0 copy-done.1
  211.6 0.3 fusion.3
  211.9 0.3 fusion.1
  212.2 0.0 copy-start
  212.2 0.9 fusion.9
  213.1 0.0 all-reduce.4.cloned.1.call-update
  213.1 82.8 %all-reduce.4.cloned.1.call-done = f32[128,128]{0,1:T(8,128)} async-done(((f32[128,128]{0,1:T(8,128)}), f32[128,128]{0,1:T(8,128)}) %all-reduce.4.cloned.1.call-update) | async-done | bytes 65552 | tf_op jit(solution)/shard_map/psum | solution.py:39
  295.9 0.9 multiply_multiply_fusion
  296.8 0.7 copy.13
  297.5 0.0 copy-done
  (5 shorter events, 0.1 us)
Async XLA Ops:
  7.2 180.6 %all-reduce.6.cloned.1.call-start = ((), (), s32[]{:S(2)}) async-start(), calls=%async_computation.1 | async-start | bytes 262144 | tf_op jit(solution)/shard_map/psum | solution.py:33
  38.0 257.9 %all-reduce.4.cloned.1.call-start = ((), (), s32[]{:S(2)}) async-start(), calls=%async_computation | async-start | bytes 131072 | tf_op jit(solution)/shard_map/psum | solution.py:39
  64.2 147.4 %copy-start.1 = (f32[64,128]{1,0:T(8,128)S(1)}, f32[64,128]{1,0:T(8,128)}, u32[]{:S(2)}) copy-start(f32[64,128]{1,0:T(8,128)} %param.7) | copy-start | bytes 98308
  212.2 85.4 %copy-start = (f32[128,64]{0,1:T(8,128)}, f32[128,64]{0,1:T(8,128)S(1)}, u32[]{:S(2)}) copy-start(f32[128,64]{0,1:T(8,128)S(1)} %fusion.1) | copy-start | bytes 98308
Sparse Core Ops, SparseCore 0:
  38.1 137.1 all-reduce.5
  213.2 82.6 all-reduce.3
where the time goes:
time: 306 us; the launch traced here: 304 us
  blocking collectives  172 us (56%)
  waiting for transfers between devices  82.8 us (27%)
  other arithmetic  30.8 us (10%)
  between operations  14.2 us (5%)
  matrix products  3.28 us (1%)
    psum x1, blocking collectives, shards(): summed = lax.psum(contraction, 'col')  117 us
    psum x1, waiting for transfers between devices, shards(): gram_a = lax.psum(gram_of(factor_a), 'row')  82.8 us
    all_gather x1, blocking collectives, shards(): lax.all_gather(factor_b, 'row', axis=1, tiled=True)  16 us
    all_gather x1, blocking collectives, shards(): lax.all_gather(delta_c, 'row', axis=1, tiled=True)  13 us
    all_gather x1, blocking collectives, shards(): lax.all_gather(factor_c, 'row', axis=1, tiled=True)  12.9 us
    all_gather x1, blocking collectives, shards(): lax.all_gather(delta_b, 'row', axis=1, tiled=True)  12.9 us
    another operation x3, other arithmetic, shards(): lower = jnp.linalg.cholesky(hadamard)  12.4 us
    another operation x2, other arithmetic, solve_rows(): jax.scipy.linalg.solve_triangular(lower, inner, lower=True, trans=1)  10.5 us
  transfers between devices with their start and end apart: 2, of which 1 were waited for; matrix products, arithmetic and copies ran while one was open for 2% of the time, Pallas kernels for 0%

commit v1 on v0

v1 whole, which is shorter than its diff:
```python
import functools

import jax
import jax.numpy as jnp
from jax import lax
from jax.experimental import pallas as pl
from jax.experimental.pallas import tpu as pltpu
from jax.sharding import PartitionSpec as P

J = 8192
K = 8192
ROWS = 512
R = 128
F32 = jnp.float32
BF16 = jnp.bfloat16
HIGH = lax.Precision.HIGHEST
MESH = pl.DeviceIdType.MESH

NX, NC, NY, NZ = 4, 2, 4, 8
ROW_OFFS = [(dx, dc) for dx in range(NX) for dc in range(NC) if dx or dc]
XY_OFFS = [(dx, dc, dy) for dy in range(NY) for dx in range(NX) for dc in range(NC) if dx or dc or dy]
GROUPS = 8


def lane_bcast(v, lane):
    return jnp.broadcast_to(v[:, lane : lane + 1], (8, R))


def sub_bcast(v, sub):
    return jnp.broadcast_to(v[sub : sub + 1, :], (8, R))


def invert(A):
    lane = lax.broadcasted_iota(jnp.int32, (8, R), 1)
    sub = lax.broadcasted_iota(jnp.int32, (8, R), 0)
    A = list(A)
    for p in range(16):
        l0 = 8 * p
        inside = (lane >= l0) & (lane < l0 + 8)
        c = [lane_bcast(A[p], l0 + i) for i in range(8)]
        rows = jnp.where(inside, jnp.where(lane - l0 == sub, 1.0, 0.0), A[p])
        for i in range(8):
            rinv = 1.0 / sub_bcast(c[i], i)
            pivot = sub_bcast(rows, i) * rinv
            rows = jnp.where(sub == i, pivot, rows - c[i] * pivot)
            for m in range(i + 1, 8):
                dr = sub_bcast(c[m], i) * rinv
                c[m] = jnp.where(sub == i, dr, c[m] - c[i] * dr)
        each = [sub_bcast(rows, i) for i in range(8)]
        for m in [(p + 1 + t) % 16 for t in range(15)]:
            a = A[m]
            t = [lane_bcast(a, l0 + i) * each[i] for i in range(8)]
            s = ((t[0] + t[1]) + (t[2] + t[3])) + ((t[4] + t[5]) + (t[6] + t[7]))
            A[m] = jnp.where(inside, 0.0, a) - s
        A[p] = rows
    return A


def kernel(
    base, opb, opc, db, dc, fb, fc, fa_out, gn_out,
    bv, cv, st_f, rv_f, rv_d, part_g, y_g, z_g, ag_g, part_m, y_m, z_m, ag_m, inv,
    op_sem, f_s, f_r, d_s, d_r, yg_s, yg_r, zg_s, zg_r, ag_s, ag_r, ym_s, ym_r, zm_s, zm_r, am_s, am_r,
):
    r, c = lax.axis_index("row"), lax.axis_index("col")
    x, core = r // 2, lax.rem(r, 2)
    z, y = c // NY, lax.rem(c, NY)

    def at_row(dx, dcore):
        return lax.rem(x + dx, NX) * 2 + lax.rem(core + dcore, NC)

    def at_col(dz, dy):
        return lax.rem(z + dz, NZ) * NY + lax.rem(y + dy, NY)

    def remote(src, dst, ss, rs, k, row, col):
        return pltpu.make_async_remote_copy(
            src_ref=src, dst_ref=dst, send_sem=ss.at[k], recv_sem=rs.at[k],
            device_id=(row, col), device_id_type=MESH)

    loads = []
    for g in range(GROUPS):
        rows = pl.ds(8 * g, 8)
        loads.append((pltpu.make_async_copy(opb.at[rows], bv.at[rows], op_sem.at[0, g]),
                      pltpu.make_async_copy(opc.at[rows], cv.at[rows], op_sem.at[1, g])))

    barrier = pltpu.get_barrier_semaphore()
    for dz in range(1, NZ):
        pl.semaphore_signal(barrier, inc=1, device_id=(r, at_col(dz, 0)), device_id_type=MESH)
    for dx, dcore, dy in reversed(XY_OFFS):
        pl.semaphore_signal(barrier, inc=1, device_id=(at_row(dx, dcore), at_col(0, dy)), device_id_type=MESH)
    for pair in loads:
        for copy in pair:
            copy.start()
    st_f[0] = fb[...]
    st_f[1] = fc[...]
    rv_d[r, :, 0:256] = db[...]
    rv_d[r, :, 256:512] = dc[...]
    rv_f[r] = st_f[core]
    pl.semaphore_wait(barrier, NZ - 1 + len(XY_OFFS))

    sent = []
    send_f, send_d = [], []
    for k, (dx, dcore) in enumerate(ROW_OFFS):
        send_f.append(remote(st_f.at[lax.rem(core + dcore, NC)], rv_f.at[r], f_s, f_r, k, at_row(dx, dcore), c))
        send_f[-1].start()
    for k, (dx, dcore) in enumerate(ROW_OFFS):
        send_d.append(remote(rv_d.at[r], rv_d.at[r], d_s, d_r, k, at_row(dx, dcore), c))
        send_d[-1].start()
    sent += send_f + send_d

    for copy in send_f:
        copy.wait_recv()
    mine = rv_f[pl.ds(2 * x, 2)].reshape(32, 256)
    gram = lax.dot_general(mine, rv_f[...].reshape(R, 256), (((1,), (1,)), ((), ())),
                           precision=HIGH, preferred_element_type=F32)
    part_g[...] = gram.reshape(NY, 8, R)
    send_yg = []
    for dy in range(1, NY):
        send_yg.append(remote(part_g.at[lax.rem(y + dy, NY)], y_g.at[dy - 1], yg_s, yg_r, dy - 1, r, at_col(0, dy)))
        send_yg[-1].start()

    for copy in send_d:
        copy.wait_recv()
    eye = lax.broadcasted_iota(jnp.int32, (R, R), 0) == lax.broadcasted_iota(jnp.int32, (R, R), 1)

    def contract(g):
        for copy in loads[g]:
            copy.wait()
        d_b = rv_d[:, :, 0:256].reshape(R, 256)
        d_c = rv_d[:, :, 256:512].reshape(R, 256)
        found = []
        for i in range(8 * g, 8 * g + 8):
            both = jnp.dot(d_b, bv[i], preferred_element_type=F32)
            both = both + jnp.dot(d_c, cv[i], preferred_element_type=F32)
            found.append(jnp.sum(jnp.where(eye, both, 0.0), axis=0, keepdims=True))
        part_m[g // 2, pl.ds(8 * (g % 2), 8), :] = jnp.concatenate(found, axis=0)

    for g in range(GROUPS // 2):
        contract(g)

    for copy in send_yg:
        copy.wait_recv()
    z_g[z] = (part_g[y] + y_g[0]) + (y_g[1] + y_g[2])
    send_zg = []
    for dz in range(1, NZ):
        send_zg.append(remote(z_g.at[z], z_g.at[z], zg_s, zg_r, dz - 1, r, at_col(dz, 0)))
        send_zg[-1].start()

    for g in range(GROUPS // 2, GROUPS):
        contract(g)
    send_ym = []
    for dy in range(1, NY):
        send_ym.append(remote(part_m.at[lax.rem(y + dy, NY)], y_m.at[dy - 1], ym_s, ym_r, dy - 1, r, at_col(0, dy)))
        send_ym[-1].start()

    for copy in send_zg:
        copy.wait_recv()
    ag_g[r, y] = ((z_g[0] + z_g[1]) + (z_g[2] + z_g[3])) + ((z_g[4] + z_g[5]) + (z_g[6] + z_g[7]))
    send_ag = []
    for k, (dx, dcore, dy) in enumerate(XY_OFFS):
        send_ag.append(remote(ag_g.at[r, y], ag_g.at[r, y], ag_s, ag_r, k, at_row(dx, dcore), at_col(0, dy)))
        send_ag[-1].start()

    for copy in send_ym:
        copy.wait_recv()
    z_m[z] = (part_m[y] + y_m[0]) + (y_m[1] + y_m[2])
    send_zm = []
    for dz in range(1, NZ):
        send_zm.append(remote(z_m.at[z], z_m.at[z], zm_s, zm_r, dz - 1, r, at_col(dz, 0)))
        send_zm[-1].start()
    for copy in send_zm:
        copy.wait_recv()
    summed = ((z_m[0] + z_m[1]) + (z_m[2] + z_m[3])) + ((z_m[4] + z_m[5]) + (z_m[6] + z_m[7]))
    ag_m[r, y] = base[pl.ds(pl.multiple_of(16 * y, 16), 16), :] + summed
    send_am = []
    for k, (dx, dcore, dy) in enumerate(XY_OFFS):
        send_am.append(remote(ag_m.at[r, y], ag_m.at[r, y], am_s, am_r, k, at_row(dx, dcore), at_col(0, dy)))
        send_am[-1].start()

    for copy in send_ag:
        copy.wait_recv()
    gathered = ag_g[...].reshape(NX, NC, 32, R)
    gram_b = gathered[:, 0].reshape(R, R)
    gram_c = gathered[:, 1].reshape(R, R) / K
    hadamard = gram_b / J * gram_c
    blocks = invert([hadamard[8 * m : 8 * m + 8, :] for m in range(16)])
    for m in range(16):
        inv[8 * m : 8 * m + 8, :] = blocks[m]

    for copy in send_am:
        copy.wait_recv()
    whole = ag_m[...].reshape(ROWS, R)
    mtm = lax.dot_general(whole, whole, (((0,), (0,)), ((), ())), precision=HIGH, preferred_element_type=F32)
    inverse = inv[...]
    own = ag_m[r].reshape(64, R)
    fa_out[...] = jnp.dot(own, inverse, precision=HIGH, preferred_element_type=F32)
    half = jnp.dot(mtm, inverse, precision=HIGH, preferred_element_type=F32)
    gram_a = lax.dot_general(inverse, half, (((0,), (0,)), ((), ())), precision=HIGH, preferred_element_type=F32)
    gn_out[...] = gram_a / ROWS * gram_c

    for copy in sent + send_yg + send_zg + send_ag + send_ym + send_zm + send_am:
        copy.wait_send()


def shards(base_mttkrp, operator_b, operator_c, delta_b, delta_c, factor_b, factor_c):
    vmem = pl.BlockSpec(memory_space=pltpu.VMEM)
    hbm = pl.BlockSpec(memory_space=pl.ANY)

    def sems(*counts):
        return [pltpu.SemaphoreType.DMA((n,)) for n in counts for _ in range(2)]

    return pl.pallas_call(
        kernel,
        out_shape=(jax.ShapeDtypeStruct((64, R), F32), jax.ShapeDtypeStruct((R, R), F32)),
        in_specs=[vmem, hbm, hbm, vmem, vmem, vmem, vmem],
        out_specs=(vmem, vmem),
        scratch_shapes=[
            pltpu.VMEM((64, 256, R), BF16),
            pltpu.VMEM((64, 256, R), BF16),
            pltpu.VMEM((2, 16, 256), F32),
            pltpu.VMEM((8, 16, 256), F32),
            pltpu.VMEM((8, 16, 512), BF16),
            pltpu.VMEM((NY, 8, R), F32),
            pltpu.VMEM((NY - 1, 8, R), F32),
            pltpu.VMEM((NZ, 8, R), F32),
            pltpu.VMEM((8, NY, 8, R), F32),
            pltpu.VMEM((NY, 16, R), F32),
            pltpu.VMEM((NY - 1, 16, R), F32),
            pltpu.VMEM((NZ, 16, R), F32),
            pltpu.VMEM((8, NY, 16, R), F32),
            pltpu.VMEM((R, R), F32),
            pltpu.SemaphoreType.DMA((2, GROUPS)),
        ] + sems(7, 7, 3, 7, 31, 3, 7, 31),
        compiler_params=pltpu.CompilerParams(
            collective_id=0, has_side_effects=True, vmem_limit_bytes=48 * 2**20),
        name="update",
    )(base_mttkrp, operator_b, operator_c, delta_b.T, delta_c.T, factor_b.T, factor_c.T)


def solution(mesh):
    return jax.shard_map(
        shards,
        mesh=mesh,
        in_specs=(
            P("row", None),
            P("row", "col", None),
            P("row", "col", None),
            P("col", "row"),
            P("col", "row"),
            P("col", "row"),
            P("col", "row"),
        ),
        out_specs=(P("row", None), P()),
        check_vma=False,
    )
```

time: 306 us -> 45.1 us (0.15)
  blocking collectives: 172 us -> 0 us
  waiting for transfers between devices: 82.8 us -> 0 us
  Pallas kernels: 0 us -> 37.1 us
  other arithmetic: 30.8 us -> 0 us
  between operations: 14.2 us -> 0.65 us
  local copies, waits for them, and re-layouts: 1.01 us -> 7.01 us
  matrix products: 3.28 us -> 0 us
    psum x1 -> x0, blocking collectives: 117 us -> none  [shards(): summed = lax.psum(contraction, 'col')]
    psum x2 -> x0, waiting for transfers between devices: 82.8 us -> none  [the longest x1 82.8 us: shards(): gram_a = lax.psum(gram_of(factor_a), 'row')]
    all_gather x4 -> x0, blocking collectives: 54.9 us -> none  [the longest x1 16 us: shards(): lax.all_gather(factor_b, 'row', axis=1, tiled=True)]
    pallas_call x0 -> x1, Pallas kernels: none -> 37.1 us  [shards(): pl.pallas_call(kernel, out_shape=(jax.ShapeDtypeStruct((64, R), F32), jax...]
    another operation x5 -> x0, other arithmetic: 22.9 us -> none  [the longest x3 12.4 us: shards(): lower = jnp.linalg.cholesky(hadamard)]
    dot_general x1 -> x0, other arithmetic: 6.13 us -> none  [shards(): jnp.einsum('ijr,jr->ir', operator_c, full_dc, preferred_element_type=jnp....]
    unnamed x7 -> x14, local copies, waits for them, and re-layouts: 0.92 us -> 7.01 us
  transfers between devices with their start and end apart: 2 -> 0, of which waited for: 1 -> 0; matrix products, arithmetic and copies ran while one was open for 2% -> 0% of each run, Pallas kernels for 0% -> 0%
where the time goes in v1:
time: 45.1 us; the launch traced here: 44.8 us
  Pallas kernels  37.1 us (82%)
  local copies, waits for them, and re-layouts  7.01 us (16%)
  between operations  0.65 us (1%)
    pallas_call x1, Pallas kernels, shards(): pl.pallas_call(kernel, out_shape=(jax.ShapeDtypeStruct((64, R), F32), jax...  37.1 us
    unnamed x14, local copies, waits for them, and re-layouts  7.01 us

profile of v1, /device:TPU:1, one launch (start us, length us, event | category | flops | bytes accessed | tf_op | source)
XLA Modules:
  0.0 44.8 jit_solution(4803135729957686881)
XLA Ops:
  0.6 0.0 copy-start
  0.6 2.2 %copy-done = bf16[64,256,128]{2,1,0:T(8,128)(2,1)S(1)} copy-done((bf16[64,256,128]{2,1,0:T(8,128)(2,1)S(1)}, bf16[64,256,128]{2,1,0:T(8,128)(2,1)}, u32[]{:S(2)}) %copy-start) | copy-done | bytes 4194328
  2.8 0.0 copy-start.1
  2.8 0.8 %copy-done.1 = f32[64,128]{1,0:T(8,128)S(1)} copy-done((f32[64,128]{1,0:T(8,128)S(1)}, f32[64,128]{1,0:T(8,128)}, u32[]{:S(2)}) %copy-start.1) | copy-done | bytes 32792
  3.6 0.0 copy-start.2
  3.6 0.7 %copy-done.2 = f32[256,16]{0,1:T(8,128)S(1)} copy-done((f32[256,16]{0,1:T(8,128)S(1)}, f32[256,16]{0,1:T(8,128)}, u32[]{:S(2)}) %copy-start.2) | copy-done | bytes 16408
  4.3 0.0 copy-start.3
  4.3 0.7 %copy-done.3 = f32[256,16]{0,1:T(8,128)S(1)} copy-done((f32[256,16]{0,1:T(8,128)S(1)}, f32[256,16]{0,1:T(8,128)}, u32[]{:S(2)}) %copy-start.3) | copy-done | bytes 16408
  5.0 0.0 copy-start.4
  5.0 0.7 %copy-done.4 = bf16[256,16]{0,1:T(8,128)(2,1)S(1)} copy-done((bf16[256,16]{0,1:T(8,128)(2,1)S(1)}, bf16[256,16]{0,1:T(8,128)(2,1)}, u32[]{:S(2)}) %copy-start.4) | copy-done | bytes 8216
  5.7 0.0 copy-start.5
  5.7 0.7 %copy-done.5 = bf16[256,16]{0,1:T(8,128)(2,1)S(1)} copy-done((bf16[256,16]{0,1:T(8,128)(2,1)S(1)}, bf16[256,16]{0,1:T(8,128)(2,1)}, u32[]{:S(2)}) %copy-start.5) | copy-done | bytes 8216
  6.4 37.1 %update.1 = (f32[64,128]{1,0:T(8,128)S(1)}, f32[128,128]{1,0:T(8,128)S(1)}) custom-call(f32[64,128]{1,0:T(8,128)S(1)} %copy-done.1, bf16[64,256,128]{2,1,0:T(8,128)(2,1)S(1)} %copy-done, bf16[64,256,128]{2,1,0:T(8,128)(2,1)} %opc.1, bf16[16,256]{1,0:T(8,128)(2,1)S(1)} %bitcast.6, bf16[16,256]{1,0:T(8,128)(2,1)S(1)} %bitcast.7, f32[16,256]{1,0:T(8,128)S(1)} %bitcast.4, ...), custom_call_target="tpu_custom_call" | custom-call | tf_op jit(solution)/shard_map/update/pallas_call | solution.py:211
  43.5 0.6 %copy.11 = f32[64,128]{1,0:T(8,128)} copy(f32[64,128]{1,0:T(8,128)S(1)} %get-tuple-element.4) | data formatting | bytes 65536
  44.1 0.6 %copy.12 = f32[128,128]{1,0:T(8,128)} copy(f32[128,128]{1,0:T(8,128)S(1)} %get-tuple-element.5) | data formatting | bytes 131072
Async XLA Ops:
  0.6 2.2 %copy-start = (bf16[64,256,128]{2,1,0:T(8,128)(2,1)S(1)}, bf16[64,256,128]{2,1,0:T(8,128)(2,1)}, u32[]{:S(2)}) copy-start(bf16[64,256,128]{2,1,0:T(8,128)(2,1)} %opb.1) | copy-start | bytes 12582916
  2.8 0.8 %copy-start.1 = (f32[64,128]{1,0:T(8,128)S(1)}, f32[64,128]{1,0:T(8,128)}, u32[]{:S(2)}) copy-start(f32[64,128]{1,0:T(8,128)} %base.1) | copy-start | bytes 98308
  3.6 0.7 %copy-start.2 = (f32[256,16]{0,1:T(8,128)S(1)}, f32[256,16]{0,1:T(8,128)}, u32[]{:S(2)}) copy-start(f32[256,16]{0,1:T(8,128)} %param.12) | copy-start | bytes 49156
  4.3 0.7 %copy-start.3 = (f32[256,16]{0,1:T(8,128)S(1)}, f32[256,16]{0,1:T(8,128)}, u32[]{:S(2)}) copy-start(f32[256,16]{0,1:T(8,128)} %param.13) | copy-start | bytes 49156
  5.0 0.7 %copy-start.4 = (bf16[256,16]{0,1:T(8,128)(2,1)S(1)}, bf16[256,16]{0,1:T(8,128)(2,1)}, u32[]{:S(2)}) copy-start(bf16[256,16]{0,1:T(8,128)(2,1)} %param.10) | copy-start | bytes 24580
  5.7 0.7 %copy-start.5 = (bf16[256,16]{0,1:T(8,128)(2,1)S(1)}, bf16[256,16]{0,1:T(8,128)(2,1)}, u32[]{:S(2)}) copy-start(bf16[256,16]{0,1:T(8,128)(2,1)} %param.11) | copy-start | bytes 24580

commit v2 on v1

--- a/solution.py
+++ b/solution.py
@@ -59,7 +59,7 @@
 def kernel(
     base, opb, opc, db, dc, fb, fc, fa_out, gn_out,
     bv, cv, st_f, rv_f, rv_d, part_g, y_g, z_g, ag_g, part_m, y_m, z_m, ag_m, inv,
-    op_sem, f_s, f_r, d_s, d_r, yg_s, yg_r, zg_s, zg_r, ag_s, ag_r, ym_s, ym_r, zm_s, zm_r, am_s, am_r,
+    base_v, in_sem, op_sem, f_s, f_r, d_s, d_r, yg_s, yg_r, zg_s, zg_r, ag_s, ag_r, ym_s, ym_r, zm_s, zm_r, am_s, am_r,
 ):
     r, c = lax.axis_index("row"), lax.axis_index("col")
     x, core = r // 2, lax.rem(r, 2)
@@ -82,6 +82,11 @@
         loads.append((pltpu.make_async_copy(opb.at[rows], bv.at[rows], op_sem.at[0, g]),
                       pltpu.make_async_copy(opc.at[rows], cv.at[rows], op_sem.at[1, g])))
 
+    small = [pltpu.make_async_copy(src, dst, in_sem.at[k]) for k, (src, dst) in enumerate((
+        (fb, st_f.at[0]), (fc, st_f.at[1]), (db, rv_d.at[r, :, pl.ds(0, 256)]),
+        (dc, rv_d.at[r, :, pl.ds(256, 256)]), (base, base_v)))]
+    for copy in small:
+        copy.start()
     barrier = pltpu.get_barrier_semaphore()
     for dz in range(1, NZ):
         pl.semaphore_signal(barrier, inc=1, device_id=(r, at_col(dz, 0)), device_id_type=MESH)
@@ -90,10 +95,8 @@
     for pair in loads:
         for copy in pair:
             copy.start()
-    st_f[0] = fb[...]
-    st_f[1] = fc[...]
-    rv_d[r, :, 0:256] = db[...]
-    rv_d[r, :, 256:512] = dc[...]
+    for copy in small:
+        copy.wait()
     rv_f[r] = st_f[core]
     pl.semaphore_wait(barrier, NZ - 1 + len(XY_OFFS))
 
@@ -170,7 +173,7 @@
     for copy in send_zm:
         copy.wait_recv()
     summed = ((z_m[0] + z_m[1]) + (z_m[2] + z_m[3])) + ((z_m[4] + z_m[5]) + (z_m[6] + z_m[7]))
-    ag_m[r, y] = base[pl.ds(pl.multiple_of(16 * y, 16), 16), :] + summed
+    ag_m[r, y] = base_v[pl.ds(pl.multiple_of(16 * y, 16), 16), :] + summed
     send_am = []
     for k, (dx, dcore, dy) in enumerate(XY_OFFS):
         send_am.append(remote(ag_m.at[r, y], ag_m.at[r, y], am_s, am_r, k, at_row(dx, dcore), at_col(0, dy)))
@@ -211,7 +214,7 @@
     return pl.pallas_call(
         kernel,
         out_shape=(jax.ShapeDtypeStruct((64, R), F32), jax.ShapeDtypeStruct((R, R), F32)),
-        in_specs=[vmem, hbm, hbm, vmem, vmem, vmem, vmem],
+        in_specs=[hbm] * 7,
         out_specs=(vmem, vmem),
         scratch_shapes=[
             pltpu.VMEM((64, 256, R), BF16),
@@ -228,10 +231,12 @@
             pltpu.VMEM((NZ, 16, R), F32),
             pltpu.VMEM((8, NY, 16, R), F32),
             pltpu.VMEM((R, R), F32),
+            pltpu.VMEM((64, R), F32),
+            pltpu.SemaphoreType.DMA((5,)),
             pltpu.SemaphoreType.DMA((2, GROUPS)),
         ] + sems(7, 7, 3, 7, 31, 3, 7, 31),
         compiler_params=pltpu.CompilerParams(
-            collective_id=0, has_side_effects=True, vmem_limit_bytes=48 * 2**20),
+            collective_id=0, has_side_effects=True, vmem_limit_bytes=60 * 2**20),
         name="update",
     )(base_mttkrp, operator_b, operator_c, delta_b.T, delta_c.T, factor_b.T, factor_c.T)
 

time: 45.1 us -> 41.8 us (0.927)
  local copies, waits for them, and re-layouts: 7.01 us -> 2.85 us
  Pallas kernels: 37.1 us -> 38.1 us
    unnamed x14 -> x2, local copies, waits for them, and re-layouts: 7.01 us -> 2.85 us
    pallas_call x1, Pallas kernels: 37.1 us -> 38.1 us  [shards(): pl.pallas_call(kernel, out_shape=(jax.ShapeDtypeStruct((64, R), F32), jax...]
where the time goes in v2:
time: 41.8 us; the launch traced here: 41.6 us
  Pallas kernels  38.1 us (91%)
  local copies, waits for them, and re-layouts  2.85 us (7%)
  between operations  0.64 us (2%)
    pallas_call x1, Pallas kernels, shards(): pl.pallas_call(kernel, out_shape=(jax.ShapeDtypeStruct((64, R), F32), jax...  38.1 us
    unnamed x2, local copies, waits for them, and re-layouts  2.85 us

profile of v2, /device:TPU:1, one launch (start us, length us, event | category | flops | bytes accessed | tf_op | source)
XLA Modules:
  0.0 41.6 jit_solution(10417241169923211792)
XLA Ops:
  0.6 38.1 %update.1 = (f32[64,128]{1,0:T(8,128)}, f32[128,128]{1,0:T(8,128)}) custom-call(f32[64,128]{1,0:T(8,128)} %base.1, bf16[64,256,128]{2,1,0:T(8,128)(2,1)} %opb.1, bf16[64,256,128]{2,1,0:T(8,128)(2,1)} %opc.1, bf16[16,256]{1,0:T(8,128)(2,1)} %bitcast.6, bf16[16,256]{1,0:T(8,128)(2,1)} %bitcast.7, f32[16,256]{1,0:T(8,128)} %bitcast.4, f32[16,256]{1,0:T(8,128)} %bitcast.5), custom_call_target="tpu_custom_call" | custom-call | tf_op jit(solution)/shard_map/update/pallas_call | solution.py:214
  38.7 1.4 %copy.11 = f32[64,128]{1,0:T(8,128)} copy(f32[64,128]{1,0:T(8,128)} %get-tuple-element.4) | data formatting | bytes 65536
  40.1 1.5 %copy.12 = f32[128,128]{1,0:T(8,128)} copy(f32[128,128]{1,0:T(8,128)} %get-tuple-element.5) | data formatting | bytes 131072

commit v3 on v2

--- a/solution.py
+++ b/solution.py
@@ -19,6 +19,7 @@
 NX, NC, NY, NZ = 4, 2, 4, 8
 ROW_OFFS = [(dx, dc) for dx in range(NX) for dc in range(NC) if dx or dc]
 XY_OFFS = [(dx, dc, dy) for dy in range(NY) for dx in range(NX) for dc in range(NC) if dx or dc or dy]
+GREETED = [(dx, dc, 0, 0) for dx, dc in reversed(ROW_OFFS)] + [(0, 0, dy, 0) for dy in (2, 1, 3)] + [(0, 0, 0, 1), (0, 0, 0, 7)]
 GROUPS = 8
 
 
@@ -34,32 +35,53 @@
     lane = lax.broadcasted_iota(jnp.int32, (8, R), 1)
     sub = lax.broadcasted_iota(jnp.int32, (8, R), 0)
     A = list(A)
-    for p in range(16):
-        l0 = 8 * p
-        inside = (lane >= l0) & (lane < l0 + 8)
-        c = [lane_bcast(A[p], l0 + i) for i in range(8)]
-        rows = jnp.where(inside, jnp.where(lane - l0 == sub, 1.0, 0.0), A[p])
-        for i in range(8):
-            rinv = 1.0 / sub_bcast(c[i], i)
-            pivot = sub_bcast(rows, i) * rinv
-            rows = jnp.where(sub == i, pivot, rows - c[i] * pivot)
-            for m in range(i + 1, 8):
-                dr = sub_bcast(c[m], i) * rinv
-                c[m] = jnp.where(sub == i, dr, c[m] - c[i] * dr)
-        each = [sub_bcast(rows, i) for i in range(8)]
-        for m in [(p + 1 + t) % 16 for t in range(15)]:
-            a = A[m]
-            t = [lane_bcast(a, l0 + i) * each[i] for i in range(8)]
-            s = ((t[0] + t[1]) + (t[2] + t[3])) + ((t[4] + t[5]) + (t[6] + t[7]))
-            A[m] = jnp.where(inside, 0.0, a) - s
-        A[p] = rows
+    for p in range(R // 16):
+        l0 = 16 * p
+        inside = (lane >= l0) & (lane < l0 + 16)
+        own = [2 * p, 2 * p + 1]
+        ahead = [m for m in (2 * p + 2, 2 * p + 3) if m < 16]
+        c = [[lane_bcast(A[u], l0 + i) for u in own] for i in range(16)]
+        early = {m: [lane_bcast(A[m], l0 + i) for i in range(16)] for m in ahead}
+        rows = [jnp.where(inside, jnp.where(lane - l0 == sub + 8 * k, 1.0, 0.0), A[u]) for k, u in enumerate(own)]
+        for i in range(0, 16, 2):
+            v, s = i // 8, i % 8
+            a, b = sub_bcast(c[i][v], s), sub_bcast(c[i + 1][v], s)
+            d, e = sub_bcast(c[i][v], s + 1), sub_bcast(c[i + 1][v], s + 1)
+            det = 1.0 / (a * e - b * d)
+            g0 = [(c[i][u] * e - c[i + 1][u] * d) * det for u in range(2)]
+            g1 = [(c[i + 1][u] * a - c[i][u] * b) * det for u in range(2)]
+            g0[v] = jnp.where(sub == s, -(e * det), jnp.where(sub == s + 1, d * det, g0[v]))
+            g1[v] = jnp.where(sub == s, b * det, jnp.where(sub == s + 1, -(a * det), g1[v]))
+            hit = (sub == s) | (sub == s + 1)
+
+            def step(t):
+                r0, r1 = sub_bcast(t[v], s), sub_bcast(t[v], s + 1)
+                kept = [jnp.where(hit, 0.0, t[u]) if u == v else t[u] for u in range(2)]
+                return [kept[u] - (g0[u] * r0 + g1[u] * r1) for u in range(2)]
+
+            for m in range(i + 2, 16):
+                c[m] = step(c[m])
+            rows = step(rows)
+        new = list(A)
+        for m in ahead:
+            t = [early[m][i] * sub_bcast(rows[i // 8], i % 8) for i in range(16)]
+            while len(t) > 1:
+                t = [t[q] + t[q + 1] for q in range(0, len(t), 2)]
+            new[m] = jnp.where(inside, 0.0, A[m]) - t[0]
+        padded = jnp.concatenate([rows[m - own[0]] if m in own else jnp.zeros((8, R), F32) for m in range(16)], axis=0)
+        update = jnp.dot(jnp.concatenate(A, axis=0), padded, precision=HIGH, preferred_element_type=F32)
+        for m in range(16):
+            if m not in own and m not in ahead:
+                new[m] = jnp.where(inside, 0.0, A[m]) - update[8 * m : 8 * m + 8]
+        new[own[0]], new[own[1]] = rows
+        A = new
     return A
 
 
 def kernel(
     base, opb, opc, db, dc, fb, fc, fa_out, gn_out,
     bv, cv, st_f, rv_f, rv_d, part_g, y_g, z_g, ag_g, part_m, y_m, z_m, ag_m, inv,
-    base_v, in_sem, op_sem, f_s, f_r, d_s, d_r, yg_s, yg_r, zg_s, zg_r, ag_s, ag_r, ym_s, ym_r, zm_s, zm_r, am_s, am_r,
+    near, far, base_v, in_sem, op_sem, f_s, f_r, d_s, d_r, yg_s, yg_r, zg_s, zg_r, ag_s, ag_r, ym_s, ym_r, zm_s, zm_r, am_s, am_r,
 ):
     r, c = lax.axis_index("row"), lax.axis_index("col")
     x, core = r // 2, lax.rem(r, 2)
@@ -88,17 +110,19 @@
     for copy in small:
         copy.start()
     barrier = pltpu.get_barrier_semaphore()
-    for dz in range(1, NZ):
-        pl.semaphore_signal(barrier, inc=1, device_id=(r, at_col(dz, 0)), device_id_type=MESH)
-    for dx, dcore, dy in reversed(XY_OFFS):
-        pl.semaphore_signal(barrier, inc=1, device_id=(at_row(dx, dcore), at_col(0, dy)), device_id_type=MESH)
+    for dx, dcore, dy, dz in GREETED:
+        pl.semaphore_signal(barrier, inc=1, device_id=(at_row(dx, dcore), at_col(dz, dy)), device_id_type=MESH)
     for pair in loads:
         for copy in pair:
             copy.start()
     for copy in small:
         copy.wait()
     rv_f[r] = st_f[core]
-    pl.semaphore_wait(barrier, NZ - 1 + len(XY_OFFS))
+    pl.semaphore_wait(barrier, len(GREETED))
+
+    def tell(sem, dz):
+        for d in (dz, NZ - dz):
+            pl.semaphore_signal(sem, inc=1, device_id=(r, at_col(d, 0)), device_id_type=MESH)
 
     sent = []
     send_f, send_d = [], []
@@ -110,6 +134,8 @@
         send_d[-1].start()
     sent += send_f + send_d
 
+    tell(near, 1)
+
     for copy in send_f:
         copy.wait_recv()
     mine = rv_f[pl.ds(2 * x, 2)].reshape(32, 256)
@@ -121,39 +147,45 @@
         send_yg.append(remote(part_g.at[lax.rem(y + dy, NY)], y_g.at[dy - 1], yg_s, yg_r, dy - 1, r, at_col(0, dy)))
         send_yg[-1].start()
 
+    pl.semaphore_wait(near, 2)
+    tell(far, 2)
     for copy in send_d:
         copy.wait_recv()
-    eye = lax.broadcasted_iota(jnp.int32, (R, R), 0) == lax.broadcasted_iota(jnp.int32, (R, R), 1)
-
-    def contract(g):
+    lanes = lax.rem(lax.broadcasted_iota(jnp.int32, (R, 2 * R), 1), R)
+    eye = lax.broadcasted_iota(jnp.int32, (R, 2 * R), 0) == lanes
+    for g in range(GROUPS):
         for copy in loads[g]:
             copy.wait()
         d_b = rv_d[:, :, 0:256].reshape(R, 256)
         d_c = rv_d[:, :, 256:512].reshape(R, 256)
         found = []
-        for i in range(8 * g, 8 * g + 8):
-            both = jnp.dot(d_b, bv[i], preferred_element_type=F32)
-            both = both + jnp.dot(d_c, cv[i], preferred_element_type=F32)
-            found.append(jnp.sum(jnp.where(eye, both, 0.0), axis=0, keepdims=True))
+        for i in range(8 * g, 8 * g + 8, 2):
+            both = jnp.dot(d_b, jnp.concatenate([bv[i], bv[i + 1]], axis=1), preferred_element_type=F32)
+            both = both + jnp.dot(d_c, jnp.concatenate([cv[i], cv[i + 1]], axis=1), preferred_element_type=F32)
+            pair = jnp.sum(jnp.where(eye, both, 0.0), axis=0, keepdims=True)
+            found += [pair[:, :R], pair[:, R:]]
         part_m[g // 2, pl.ds(8 * (g % 2), 8), :] = jnp.concatenate(found, axis=0)
-
-    for g in range(GROUPS // 2):
-        contract(g)
+    send_ym = []
+    for dy in range(1, NY):
+        send_ym.append(remote(part_m.at[lax.rem(y + dy, NY)], y_m.at[dy - 1], ym_s, ym_r, dy - 1, r, at_col(0, dy)))
+        send_ym[-1].start()
 
     for copy in send_yg:
         copy.wait_recv()
     z_g[z] = (part_g[y] + y_g[0]) + (y_g[1] + y_g[2])
+    pl.semaphore_wait(far, 2)
     send_zg = []
     for dz in range(1, NZ):
         send_zg.append(remote(z_g.at[z], z_g.at[z], zg_s, zg_r, dz - 1, r, at_col(dz, 0)))
         send_zg[-1].start()
 
-    for g in range(GROUPS // 2, GROUPS):
-        contract(g)
-    send_ym = []
-    for dy in range(1, NY):
-        send_ym.append(remote(part_m.at[lax.rem(y + dy, NY)], y_m.at[dy - 1], ym_s, ym_r, dy - 1, r, at_col(0, dy)))
-        send_ym[-1].start()
+    for copy in send_ym:
+        copy.wait_recv()
+    z_m[z] = (part_m[y] + y_m[0]) + (y_m[1] + y_m[2])
+    send_zm = []
+    for dz in range(1, NZ):
+        send_zm.append(remote(z_m.at[z], z_m.at[z], zm_s, zm_r, dz - 1, r, at_col(dz, 0)))
+        send_zm[-1].start()
 
     for copy in send_zg:
         copy.wait_recv()
@@ -163,13 +195,6 @@
         send_ag.append(remote(ag_g.at[r, y], ag_g.at[r, y], ag_s, ag_r, k, at_row(dx, dcore), at_col(0, dy)))
         send_ag[-1].start()
 
-    for copy in send_ym:
-        copy.wait_recv()
-    z_m[z] = (part_m[y] + y_m[0]) + (y_m[1] + y_m[2])
-    send_zm = []
-    for dz in range(1, NZ):
-        send_zm.append(remote(z_m.at[z], z_m.at[z], zm_s, zm_r, dz - 1, r, at_col(dz, 0)))
-        send_zm[-1].start()
     for copy in send_zm:
         copy.wait_recv()
     summed = ((z_m[0] + z_m[1]) + (z_m[2] + z_m[3])) + ((z_m[4] + z_m[5]) + (z_m[6] + z_m[7]))
@@ -205,15 +230,16 @@
 
 
 def shards(base_mttkrp, operator_b, operator_c, delta_b, delta_c, factor_b, factor_c):
+    args = (base_mttkrp, operator_b, operator_c, delta_b.T, delta_c.T, factor_b.T, factor_c.T)
     vmem = pl.BlockSpec(memory_space=pltpu.VMEM)
-    hbm = pl.BlockSpec(memory_space=pl.ANY)
+    hbm = pl.BlockSpec(memory_space=pltpu.HBM)
 
     def sems(*counts):
         return [pltpu.SemaphoreType.DMA((n,)) for n in counts for _ in range(2)]
 
     return pl.pallas_call(
         kernel,
-        out_shape=(jax.ShapeDtypeStruct((64, R), F32), jax.ShapeDtypeStruct((R, R), F32)),
+        out_shape=(pltpu.VMEM((64, R), F32), pltpu.VMEM((R, R), F32)),
         in_specs=[hbm] * 7,
         out_specs=(vmem, vmem),
         scratch_shapes=[
@@ -231,14 +257,16 @@
             pltpu.VMEM((NZ, 16, R), F32),
             pltpu.VMEM((8, NY, 16, R), F32),
             pltpu.VMEM((R, R), F32),
+            pltpu.SemaphoreType.REGULAR,
+            pltpu.SemaphoreType.REGULAR,
             pltpu.VMEM((64, R), F32),
             pltpu.SemaphoreType.DMA((5,)),
             pltpu.SemaphoreType.DMA((2, GROUPS)),
         ] + sems(7, 7, 3, 7, 31, 3, 7, 31),
         compiler_params=pltpu.CompilerParams(
-            collective_id=0, has_side_effects=True, vmem_limit_bytes=60 * 2**20),
+            collective_id=0, has_side_effects=True, vmem_limit_bytes=40 * 2**20),
         name="update",
-    )(base_mttkrp, operator_b, operator_c, delta_b.T, delta_c.T, factor_b.T, factor_c.T)
+    )(*(pltpu.with_memory_space_constraint(a, pltpu.HBM) for a in args))
 
 
 def solution(mesh):

time: 41.8 us -> 36.5 us (0.87)
  Pallas kernels: 38.1 us -> 34.4 us
  local copies, waits for them, and re-layouts: 2.85 us -> 1.25 us
    pallas_call x1, Pallas kernels: 38.1 us -> 34.4 us  [shards(): pl.pallas_call(kernel, out_shape=(pltpu.VMEM((64, R), F32), pltpu.VMEM((R...]
    unnamed x2, local copies, waits for them, and re-layouts: 2.85 us -> 1.25 us
where the time goes in v3:
time: 36.5 us; the launch traced here: 36.3 us
  Pallas kernels  34.4 us (94%)
  local copies, waits for them, and re-layouts  1.25 us (3%)
  between operations  0.64 us (2%)
    pallas_call x1, Pallas kernels, shards(): pl.pallas_call(kernel, out_shape=(pltpu.VMEM((64, R), F32), pltpu.VMEM((R...  34.4 us
    unnamed x2, local copies, waits for them, and re-layouts  1.25 us

profile of v3, /device:TPU:1, one launch (start us, length us, event | category | flops | bytes accessed | tf_op | source)
XLA Modules:
  0.0 36.3 jit_solution(3877984254934380283)
XLA Ops:
  0.6 34.4 %update.1 = (f32[64,128]{1,0:T(8,128)S(1)}, f32[128,128]{1,0:T(8,128)S(1)}) custom-call(f32[64,128]{1,0:T(8,128)} %base.1, bf16[64,256,128]{2,1,0:T(8,128)(2,1)} %opb.1, bf16[64,256,128]{2,1,0:T(8,128)(2,1)} %opc.1, bf16[16,256]{1,0:T(8,128)(2,1)} %bitcast.6, bf16[16,256]{1,0:T(8,128)(2,1)} %bitcast.7, f32[16,256]{1,0:T(8,128)} %bitcast.4, f32[16,256]{1,0:T(8,128)} %bitcast.5), custom_call_target="tpu_custom_call" | custom-call | tf_op jit(solution)/shard_map/update/pallas_call | solution.py:240
  35.1 0.6 %copy.11 = f32[64,128]{1,0:T(8,128)} copy(f32[64,128]{1,0:T(8,128)S(1)} %get-tuple-element.2) | data formatting | bytes 65536
  35.7 0.6 %copy.12 = f32[128,128]{1,0:T(8,128)} copy(f32[128,128]{1,0:T(8,128)S(1)} %get-tuple-element.3) | data formatting | bytes 131072

commit v4 on v3

--- a/solution.py
+++ b/solution.py
@@ -17,9 +17,12 @@
 MESH = pl.DeviceIdType.MESH
 
 NX, NC, NY, NZ = 4, 2, 4, 8
-ROW_OFFS = [(dx, dc) for dx in range(NX) for dc in range(NC) if dx or dc]
+ROW_OFFS = [(2, 1), (1, 1), (3, 1), (2, 0), (1, 0), (3, 0), (0, 1)]
 XY_OFFS = [(dx, dc, dy) for dy in range(NY) for dx in range(NX) for dc in range(NC) if dx or dc or dy]
-GREETED = [(dx, dc, 0, 0) for dx, dc in reversed(ROW_OFFS)] + [(0, 0, dy, 0) for dy in (2, 1, 3)] + [(0, 0, 0, 1), (0, 0, 0, 7)]
+GREETED = [(dx, dc, 0, 0) for dx, dc in ROW_OFFS[:4]] + [(0, 0, 2, 0)] + [(dx, dc, 0, 0) for dx, dc in ROW_OFFS[4:]] + [(0, 0, 1, 0), (0, 0, 3, 0), (0, 0, 0, 1), (0, 0, 0, 7)]
+SAME_CORE = sorted([(dx, dy) for dx in range(NX) for dy in range(NY) if dx or dy], key=lambda o: -(min(o[0], 4 - o[0]) + min(o[1], 4 - o[1])))
+HOOK = 6
+CHUNKS = 2
 GROUPS = 8
 
 
@@ -31,11 +34,12 @@
     return jnp.broadcast_to(v[sub : sub + 1, :], (8, R))
 
 
-def invert(A):
+def invert(A, between):
     lane = lax.broadcasted_iota(jnp.int32, (8, R), 1)
     sub = lax.broadcasted_iota(jnp.int32, (8, R), 0)
     A = list(A)
     for p in range(R // 16):
+        between(p)
         l0 = 16 * p
         inside = (lane >= l0) & (lane < l0 + 16)
         own = [2 * p, 2 * p + 1]
@@ -80,8 +84,8 @@
 
 def kernel(
     base, opb, opc, db, dc, fb, fc, fa_out, gn_out,
-    bv, cv, st_f, rv_f, rv_d, part_g, y_g, z_g, ag_g, part_m, y_m, z_m, ag_m, inv,
-    near, far, base_v, in_sem, op_sem, f_s, f_r, d_s, d_r, yg_s, yg_r, zg_s, zg_r, ag_s, ag_r, ym_s, ym_r, zm_s, zm_r, am_s, am_r,
+    bv, cv, st_f, rv_f, rv_d, part_g, y_g, z_g, ag_g, part_m, y_m, z_m, ag_m, mtm_v, inv,
+    near, far, base_v, in_sem, op_sem, f_s, f_r, d_s, d_r, yg_s, yg_r, zg_s, zg_r, ag_s, ag_r, ym_s, ym_r, zm_s, zm_r, am_s, am_r, mt_s, mt_r,
 ):
     r, c = lax.axis_index("row"), lax.axis_index("col")
     x, core = r // 2, lax.rem(r, 2)
@@ -99,22 +103,19 @@
             device_id=(row, col), device_id_type=MESH)
 
     loads = []
-    for g in range(GROUPS):
-        rows = pl.ds(8 * g, 8)
+    for g in range(CHUNKS):
+        rows = pl.ds(64 // CHUNKS * g, 64 // CHUNKS)
         loads.append((pltpu.make_async_copy(opb.at[rows], bv.at[rows], op_sem.at[0, g]),
                       pltpu.make_async_copy(opc.at[rows], cv.at[rows], op_sem.at[1, g])))
 
     small = [pltpu.make_async_copy(src, dst, in_sem.at[k]) for k, (src, dst) in enumerate((
         (fb, st_f.at[0]), (fc, st_f.at[1]), (db, rv_d.at[r, :, pl.ds(0, 256)]),
         (dc, rv_d.at[r, :, pl.ds(256, 256)]), (base, base_v)))]
-    for copy in small:
-        copy.start()
     barrier = pltpu.get_barrier_semaphore()
     for dx, dcore, dy, dz in GREETED:
         pl.semaphore_signal(barrier, inc=1, device_id=(at_row(dx, dcore), at_col(dz, dy)), device_id_type=MESH)
-    for pair in loads:
-        for copy in pair:
-            copy.start()
+    for copy in small:
+        copy.start()
     for copy in small:
         copy.wait()
     rv_f[r] = st_f[core]
@@ -135,6 +136,9 @@
     sent += send_f + send_d
 
     tell(near, 1)
+    for pair in loads:
+        for copy in pair:
+            copy.start()
 
     for copy in send_f:
         copy.wait_recv()
@@ -143,7 +147,7 @@
                            precision=HIGH, preferred_element_type=F32)
     part_g[...] = gram.reshape(NY, 8, R)
     send_yg = []
-    for dy in range(1, NY):
+    for dy in (2, 1, 3):
         send_yg.append(remote(part_g.at[lax.rem(y + dy, NY)], y_g.at[dy - 1], yg_s, yg_r, dy - 1, r, at_col(0, dy)))
         send_yg[-1].start()
 
@@ -154,8 +158,9 @@
     lanes = lax.rem(lax.broadcasted_iota(jnp.int32, (R, 2 * R), 1), R)
     eye = lax.broadcasted_iota(jnp.int32, (R, 2 * R), 0) == lanes
     for g in range(GROUPS):
-        for copy in loads[g]:
-            copy.wait()
+        if g % (GROUPS // CHUNKS) == 0:
+            for copy in loads[g // (GROUPS // CHUNKS)]:
+                copy.wait()
         d_b = rv_d[:, :, 0:256].reshape(R, 256)
         d_c = rv_d[:, :, 256:512].reshape(R, 256)
         found = []
@@ -166,7 +171,7 @@
             found += [pair[:, :R], pair[:, R:]]
         part_m[g // 2, pl.ds(8 * (g % 2), 8), :] = jnp.concatenate(found, axis=0)
     send_ym = []
-    for dy in range(1, NY):
+    for dy in (2, 1, 3):
         send_ym.append(remote(part_m.at[lax.rem(y + dy, NY)], y_m.at[dy - 1], ym_s, ym_r, dy - 1, r, at_col(0, dy)))
         send_ym[-1].start()
 
@@ -175,7 +180,7 @@
     z_g[z] = (part_g[y] + y_g[0]) + (y_g[1] + y_g[2])
     pl.semaphore_wait(far, 2)
     send_zg = []
-    for dz in range(1, NZ):
+    for dz in (4, 3, 5, 2, 6, 1, 7):
         send_zg.append(remote(z_g.at[z], z_g.at[z], zg_s, zg_r, dz - 1, r, at_col(dz, 0)))
         send_zg[-1].start()
 
@@ -183,49 +188,66 @@
         copy.wait_recv()
     z_m[z] = (part_m[y] + y_m[0]) + (y_m[1] + y_m[2])
     send_zm = []
-    for dz in range(1, NZ):
+    for dz in (4, 3, 5, 2, 6, 1, 7):
         send_zm.append(remote(z_m.at[z], z_m.at[z], zm_s, zm_r, dz - 1, r, at_col(dz, 0)))
         send_zm[-1].start()
 
     for copy in send_zg:
         copy.wait_recv()
-    ag_g[r, y] = ((z_g[0] + z_g[1]) + (z_g[2] + z_g[3])) + ((z_g[4] + z_g[5]) + (z_g[6] + z_g[7]))
+    ag_g[x, core, y] = ((z_g[0] + z_g[1]) + (z_g[2] + z_g[3])) + ((z_g[4] + z_g[5]) + (z_g[6] + z_g[7]))
     send_ag = []
-    for k, (dx, dcore, dy) in enumerate(XY_OFFS):
-        send_ag.append(remote(ag_g.at[r, y], ag_g.at[r, y], ag_s, ag_r, k, at_row(dx, dcore), at_col(0, dy)))
+    for k, (dx, dy) in enumerate(SAME_CORE):
+        send_ag.append(remote(ag_g.at[x, core, y], ag_g.at[x, core, y], ag_s, ag_r, k, at_row(dx, 0), at_col(0, dy)))
         send_ag[-1].start()
 
     for copy in send_zm:
         copy.wait_recv()
     summed = ((z_m[0] + z_m[1]) + (z_m[2] + z_m[3])) + ((z_m[4] + z_m[5]) + (z_m[6] + z_m[7]))
-    ag_m[r, y] = base_v[pl.ds(pl.multiple_of(16 * y, 16), 16), :] + summed
+    ag_m[x, y] = base_v[pl.ds(pl.multiple_of(16 * y, 16), 16), :] + summed
     send_am = []
-    for k, (dx, dcore, dy) in enumerate(XY_OFFS):
-        send_am.append(remote(ag_m.at[r, y], ag_m.at[r, y], am_s, am_r, k, at_row(dx, dcore), at_col(0, dy)))
+    for k, (dx, dy) in enumerate(SAME_CORE):
+        send_am.append(remote(ag_m.at[x, y], ag_m.at[x, y], am_s, am_r, k, at_row(dx, 0), at_col(0, dy)))
         send_am[-1].start()
 
+    for copy in sent + send_yg + send_zg + send_ym:
+        copy.wait_send()
     for copy in send_ag:
         copy.wait_recv()
+    over_g = remote(ag_g.at[:, core], ag_g.at[:, core], ag_s, ag_r, 15, at_row(0, 1), c)
+    over_g.start()
+    over_g.wait_recv()
+    for copy in send_ag + send_zm:
+        copy.wait_send()
     gathered = ag_g[...].reshape(NX, NC, 32, R)
     gram_b = gathered[:, 0].reshape(R, R)
     gram_c = gathered[:, 1].reshape(R, R) / K
     hadamard = gram_b / J * gram_c
-    blocks = invert([hadamard[8 * m : 8 * m + 8, :] for m in range(16)])
+    whole_sum = []
+
+    def between(panel):
+        if panel != HOOK:
+            return
+        for copy in send_am:
+            copy.wait_recv()
+        whole = ag_m[...].reshape(ROWS // 2, R)
+        mtm_v[core] = lax.dot_general(whole, whole, (((0,), (0,)), ((), ())), precision=HIGH, preferred_element_type=F32)
+        whole_sum.append(remote(mtm_v.at[core], mtm_v.at[core], mt_s, mt_r, 0, at_row(0, 1), c))
+        whole_sum[0].start()
+
+    blocks = invert([hadamard[8 * m : 8 * m + 8, :] for m in range(16)], between)
     for m in range(16):
         inv[8 * m : 8 * m + 8, :] = blocks[m]
-
-    for copy in send_am:
-        copy.wait_recv()
-    whole = ag_m[...].reshape(ROWS, R)
-    mtm = lax.dot_general(whole, whole, (((0,), (0,)), ((), ())), precision=HIGH, preferred_element_type=F32)
+    swap, = whole_sum
+    swap.wait_recv()
+    mtm = mtm_v[0] + mtm_v[1]
     inverse = inv[...]
-    own = ag_m[r].reshape(64, R)
+    own = ag_m[x].reshape(64, R)
     fa_out[...] = jnp.dot(own, inverse, precision=HIGH, preferred_element_type=F32)
     half = jnp.dot(mtm, inverse, precision=HIGH, preferred_element_type=F32)
     gram_a = lax.dot_general(inverse, half, (((0,), (0,)), ((), ())), precision=HIGH, preferred_element_type=F32)
     gn_out[...] = gram_a / ROWS * gram_c
 
-    for copy in sent + send_yg + send_zg + send_ag + send_ym + send_zm + send_am:
+    for copy in send_am + [swap, over_g]:
         copy.wait_send()
 
 
@@ -251,18 +273,19 @@
             pltpu.VMEM((NY, 8, R), F32),
             pltpu.VMEM((NY - 1, 8, R), F32),
             pltpu.VMEM((NZ, 8, R), F32),
-            pltpu.VMEM((8, NY, 8, R), F32),
+            pltpu.VMEM((NX, NC, NY, 8, R), F32),
             pltpu.VMEM((NY, 16, R), F32),
             pltpu.VMEM((NY - 1, 16, R), F32),
             pltpu.VMEM((NZ, 16, R), F32),
-            pltpu.VMEM((8, NY, 16, R), F32),
+            pltpu.VMEM((NX, NY, 16, R), F32),
+            pltpu.VMEM((NC, R, R), F32),
             pltpu.VMEM((R, R), F32),
             pltpu.SemaphoreType.REGULAR,
             pltpu.SemaphoreType.REGULAR,
             pltpu.VMEM((64, R), F32),
             pltpu.SemaphoreType.DMA((5,)),
-            pltpu.SemaphoreType.DMA((2, GROUPS)),
-        ] + sems(7, 7, 3, 7, 31, 3, 7, 31),
+            pltpu.SemaphoreType.DMA((2, CHUNKS)),
+        ] + sems(7, 7, 3, 7, 16, 3, 7, 15, 1),
         compiler_params=pltpu.CompilerParams(
             collective_id=0, has_side_effects=True, vmem_limit_bytes=40 * 2**20),
         name="update",

time: 36.5 us -> 35.5 us (0.973)
  Pallas kernels: 34.4 us -> 33.4 us
    pallas_call x1, Pallas kernels: 34.4 us -> 33.4 us  [shards(): pl.pallas_call(kernel, out_shape=(pltpu.VMEM((64, R), F32), pltpu.VMEM((R...]
where the time goes in v4:
time: 35.5 us; the launch traced here: 35.3 us
  Pallas kernels  33.4 us (94%)
  local copies, waits for them, and re-layouts  1.25 us (4%)
  between operations  0.64 us (2%)
    pallas_call x1, Pallas kernels, shards(): pl.pallas_call(kernel, out_shape=(pltpu.VMEM((64, R), F32), pltpu.VMEM((R...  33.4 us
    unnamed x2, local copies, waits for them, and re-layouts  1.25 us

profile of v4, /device:TPU:1, one launch (start us, length us, event | category | flops | bytes accessed | tf_op | source)
XLA Modules:
  0.0 35.3 jit_solution(9076622266089702151)
XLA Ops:
  0.6 33.4 %update.1 = (f32[64,128]{1,0:T(8,128)S(1)}, f32[128,128]{1,0:T(8,128)S(1)}) custom-call(f32[64,128]{1,0:T(8,128)} %base.1, bf16[64,256,128]{2,1,0:T(8,128)(2,1)} %opb.1, bf16[64,256,128]{2,1,0:T(8,128)(2,1)} %opc.1, bf16[16,256]{1,0:T(8,128)(2,1)} %bitcast.6, bf16[16,256]{1,0:T(8,128)(2,1)} %bitcast.7, f32[16,256]{1,0:T(8,128)} %bitcast.4, f32[16,256]{1,0:T(8,128)} %bitcast.5), custom_call_target="tpu_custom_call" | custom-call | tf_op jit(solution)/shard_map/update/pallas_call | solution.py:262
  34.1 0.6 %copy.11 = f32[64,128]{1,0:T(8,128)} copy(f32[64,128]{1,0:T(8,128)S(1)} %get-tuple-element.2) | data formatting | bytes 65536
  34.7 0.6 %copy.12 = f32[128,128]{1,0:T(8,128)} copy(f32[128,128]{1,0:T(8,128)S(1)} %get-tuple-element.3) | data formatting | bytes 131072

commit v5 on v4

--- a/solution.py
+++ b/solution.py
@@ -17,9 +17,8 @@
 MESH = pl.DeviceIdType.MESH
 
 NX, NC, NY, NZ = 4, 2, 4, 8
-ROW_OFFS = [(2, 1), (1, 1), (3, 1), (2, 0), (1, 0), (3, 0), (0, 1)]
 XY_OFFS = [(dx, dc, dy) for dy in range(NY) for dx in range(NX) for dc in range(NC) if dx or dc or dy]
-GREETED = [(dx, dc, 0, 0) for dx, dc in ROW_OFFS[:4]] + [(0, 0, 2, 0)] + [(dx, dc, 0, 0) for dx, dc in ROW_OFFS[4:]] + [(0, 0, 1, 0), (0, 0, 3, 0), (0, 0, 0, 1), (0, 0, 0, 7)]
+GREETED = [(2, 0, 0, 0), (0, 0, 2, 0), (1, 0, 0, 0), (3, 0, 0, 0), (0, 0, 1, 0), (0, 0, 3, 0), (0, 0, 0, 1), (0, 0, 0, 7), (0, 1, 0, 0)]
 SAME_CORE = sorted([(dx, dy) for dx in range(NX) for dy in range(NY) if dx or dy], key=lambda o: -(min(o[0], 4 - o[0]) + min(o[1], 4 - o[1])))
 HOOK = 6
 CHUNKS = 2
@@ -84,8 +83,8 @@
 
 def kernel(
     base, opb, opc, db, dc, fb, fc, fa_out, gn_out,
-    bv, cv, st_f, rv_f, rv_d, part_g, y_g, z_g, ag_g, part_m, y_m, z_m, ag_m, mtm_v, inv,
-    near, far, base_v, in_sem, op_sem, f_s, f_r, d_s, d_r, yg_s, yg_r, zg_s, zg_r, ag_s, ag_r, ym_s, ym_r, zm_s, zm_r, am_s, am_r, mt_s, mt_r,
+    bv, cv, st_f, pass_f, rv_f, rv_d, part_g, y_g, z_g, ag_g, part_m, y_m, z_m, ag_m, mtm_v, inv,
+    near, far, base_v, in_sem, op_sem, p_s, p_r, f_s, f_r, d_s, d_r, yg_s, yg_r, zg_s, zg_r, ag_s, ag_r, ym_s, ym_r, zm_s, zm_r, am_s, am_r, mt_s, mt_r,
 ):
     r, c = lax.axis_index("row"), lax.axis_index("col")
     x, core = r // 2, lax.rem(r, 2)
@@ -109,8 +108,8 @@
                       pltpu.make_async_copy(opc.at[rows], cv.at[rows], op_sem.at[1, g])))
 
     small = [pltpu.make_async_copy(src, dst, in_sem.at[k]) for k, (src, dst) in enumerate((
-        (fb, st_f.at[0]), (fc, st_f.at[1]), (db, rv_d.at[r, :, pl.ds(0, 256)]),
-        (dc, rv_d.at[r, :, pl.ds(256, 256)]), (base, base_v)))]
+        (fb, st_f.at[0]), (fc, st_f.at[1]), (db, rv_d.at[x, core, :, pl.ds(0, 256)]),
+        (dc, rv_d.at[x, core, :, pl.ds(256, 256)]), (base, base_v)))]
     barrier = pltpu.get_barrier_semaphore()
     for dx, dcore, dy, dz in GREETED:
         pl.semaphore_signal(barrier, inc=1, device_id=(at_row(dx, dcore), at_col(dz, dy)), device_id_type=MESH)
@@ -118,7 +117,8 @@
         copy.start()
     for copy in small:
         copy.wait()
-    rv_f[r] = st_f[core]
+    rv_f[x, core] = st_f[core]
+    pass_f[x] = st_f[1 - core]
     pl.semaphore_wait(barrier, len(GREETED))
 
     def tell(sem, dz):
@@ -126,23 +126,33 @@
             pl.semaphore_signal(sem, inc=1, device_id=(r, at_col(d, 0)), device_id_type=MESH)
 
     sent = []
-    send_f, send_d = [], []
-    for k, (dx, dcore) in enumerate(ROW_OFFS):
-        send_f.append(remote(st_f.at[lax.rem(core + dcore, NC)], rv_f.at[r], f_s, f_r, k, at_row(dx, dcore), c))
+    pass_in, send_f, send_d = [], [], []
+    for k, dx in enumerate((2, 1, 3)):
+        pass_in.append(remote(st_f.at[1 - core], pass_f.at[x], p_s, p_r, k, at_row(dx, 0), c))
+        pass_in[-1].start()
+    for k, dx in enumerate((2, 1, 3)):
+        send_d.append(remote(rv_d.at[x, core], rv_d.at[x, core], d_s, d_r, k, at_row(dx, 0), c))
+        send_d[-1].start()
+    for k, dx in enumerate((2, 1, 3)):
+        send_f.append(remote(st_f.at[core], rv_f.at[x, core], f_s, f_r, k, at_row(dx, 0), c))
         send_f[-1].start()
-    for k, (dx, dcore) in enumerate(ROW_OFFS):
-        send_d.append(remote(rv_d.at[r], rv_d.at[r], d_s, d_r, k, at_row(dx, dcore), c))
-        send_d[-1].start()
-    sent += send_f + send_d
-
     tell(near, 1)
     for pair in loads:
         for copy in pair:
             copy.start()
 
-    for copy in send_f:
-        copy.wait_recv()
-    mine = rv_f[pl.ds(2 * x, 2)].reshape(32, 256)
+    for copy in pass_in:
+        copy.wait_recv()
+    over_f = remote(pass_f, rv_f.at[:, core], f_s, f_r, 3, at_row(0, 1), c)
+    over_f.start()
+
+    for copy in send_d:
+        copy.wait_recv()
+    over_d = remote(rv_d.at[:, core], rv_d.at[:, core], d_s, d_r, 3, at_row(0, 1), c)
+    over_d.start()
+    for copy in send_f + [over_f]:
+        copy.wait_recv()
+    mine = rv_f[x].reshape(32, 256)
     gram = lax.dot_general(mine, rv_f[...].reshape(R, 256), (((1,), (1,)), ((), ())),
                            precision=HIGH, preferred_element_type=F32)
     part_g[...] = gram.reshape(NY, 8, R)
@@ -153,16 +163,16 @@
 
     pl.semaphore_wait(near, 2)
     tell(far, 2)
-    for copy in send_d:
-        copy.wait_recv()
+    over_d.wait_recv()
+    sent += pass_in + send_f + send_d + [over_f, over_d]
     lanes = lax.rem(lax.broadcasted_iota(jnp.int32, (R, 2 * R), 1), R)
     eye = lax.broadcasted_iota(jnp.int32, (R, 2 * R), 0) == lanes
     for g in range(GROUPS):
         if g % (GROUPS // CHUNKS) == 0:
             for copy in loads[g // (GROUPS // CHUNKS)]:
                 copy.wait()
-        d_b = rv_d[:, :, 0:256].reshape(R, 256)
-        d_c = rv_d[:, :, 256:512].reshape(R, 256)
+        d_b = rv_d[:, :, :, 0:256].reshape(R, 256)
+        d_c = rv_d[:, :, :, 256:512].reshape(R, 256)
         found = []
         for i in range(8 * g, 8 * g + 8, 2):
             both = jnp.dot(d_b, jnp.concatenate([bv[i], bv[i + 1]], axis=1), preferred_element_type=F32)
@@ -251,6 +261,14 @@
         copy.wait_send()
 
 
+def deliver(fa, gn, fa_out, gn_out, sem):
+    copies = [pltpu.make_async_copy(src, dst, sem.at[k]) for k, (src, dst) in enumerate(((fa, fa_out), (gn, gn_out)))]
+    for copy in copies:
+        copy.start()
+    for copy in copies:
+        copy.wait()
+
+
 def shards(base_mttkrp, operator_b, operator_c, delta_b, delta_c, factor_b, factor_c):
     args = (base_mttkrp, operator_b, operator_c, delta_b.T, delta_c.T, factor_b.T, factor_c.T)
     vmem = pl.BlockSpec(memory_space=pltpu.VMEM)
@@ -259,7 +277,7 @@
     def sems(*counts):
         return [pltpu.SemaphoreType.DMA((n,)) for n in counts for _ in range(2)]
 
-    return pl.pallas_call(
+    solved = pl.pallas_call(
         kernel,
         out_shape=(pltpu.VMEM((64, R), F32), pltpu.VMEM((R, R), F32)),
         in_specs=[hbm] * 7,
@@ -268,8 +286,9 @@
             pltpu.VMEM((64, 256, R), BF16),
             pltpu.VMEM((64, 256, R), BF16),
             pltpu.VMEM((2, 16, 256), F32),
-            pltpu.VMEM((8, 16, 256), F32),
-            pltpu.VMEM((8, 16, 512), BF16),
+            pltpu.VMEM((NX, 16, 256), F32),
+            pltpu.VMEM((NX, NC, 16, 256), F32),
+            pltpu.VMEM((NX, NC, 16, 512), BF16),
             pltpu.VMEM((NY, 8, R), F32),
             pltpu.VMEM((NY - 1, 8, R), F32),
             pltpu.VMEM((NZ, 8, R), F32),
@@ -285,11 +304,19 @@
             pltpu.VMEM((64, R), F32),
             pltpu.SemaphoreType.DMA((5,)),
             pltpu.SemaphoreType.DMA((2, CHUNKS)),
-        ] + sems(7, 7, 3, 7, 16, 3, 7, 15, 1),
+        ] + sems(3, 4, 4, 3, 7, 16, 3, 7, 15, 1),
         compiler_params=pltpu.CompilerParams(
             collective_id=0, has_side_effects=True, vmem_limit_bytes=40 * 2**20),
         name="update",
     )(*(pltpu.with_memory_space_constraint(a, pltpu.HBM) for a in args))
+    return pl.pallas_call(
+        deliver,
+        out_shape=(jax.ShapeDtypeStruct((64, R), F32), jax.ShapeDtypeStruct((R, R), F32)),
+        in_specs=[vmem] * 2,
+        out_specs=(hbm, hbm),
+        scratch_shapes=[pltpu.SemaphoreType.DMA((2,))],
+        name="deliver",
+    )(*(pltpu.with_memory_space_constraint(a, pltpu.VMEM) for a in solved))
 
 
 def solution(mesh):

time: 35.5 us -> 34.5 us (0.972)
  local copies, waits for them, and re-layouts: 1.25 us -> 0 us
    unnamed x2 -> x0, local copies, waits for them, and re-layouts: 1.25 us -> none
    pallas_call x0 -> x1, Pallas kernels: none -> 0.66 us  [shards(): pl.pallas_call(deliver, out_shape=(jax.ShapeDtypeStruct((64, R), F32), ja...]
    pallas_call x1, Pallas kernels: 33.4 us -> 33 us  [shards(): pl.pallas_call(kernel, out_shape=(pltpu.VMEM((64, R), F32), pltpu.VMEM((R...]
where the time goes in v5:
time: 34.5 us; the launch traced here: 34.3 us
  Pallas kernels  33.7 us (98%)
  between operations  0.64 us (2%)
    pallas_call x1, Pallas kernels, shards(): pl.pallas_call(kernel, out_shape=(pltpu.VMEM((64, R), F32), pltpu.VMEM((R...  33 us

profile of v5, /device:TPU:1, one launch (start us, length us, event | category | flops | bytes accessed | tf_op | source)
XLA Modules:
  0.0 34.3 jit_solution(12272568962179305615)
XLA Ops:
  0.6 33.0 %update.1 = (f32[64,128]{1,0:T(8,128)S(1)}, f32[128,128]{1,0:T(8,128)S(1)}) custom-call(f32[64,128]{1,0:T(8,128)} %base.1, bf16[64,256,128]{2,1,0:T(8,128)(2,1)} %opb.1, bf16[64,256,128]{2,1,0:T(8,128)(2,1)} %opc.1, bf16[16,256]{1,0:T(8,128)(2,1)} %bitcast.6, bf16[16,256]{1,0:T(8,128)(2,1)} %bitcast.7, f32[16,256]{1,0:T(8,128)} %bitcast.4, f32[16,256]{1,0:T(8,128)} %bitcast.5), custom_call_target="tpu_custom_call" | custom-call | tf_op jit(solution)/shard_map/update/pallas_call | solution.py:280
  33.6 0.7 %deliver.1 = (f32[64,128]{1,0:T(8,128)}, f32[128,128]{1,0:T(8,128)}) custom-call(f32[64,128]{1,0:T(8,128)S(1)} %get-tuple-element.4.fa, f32[128,128]{1,0:T(8,128)S(1)} %get-tuple-element.5.gn), custom_call_target="tpu_custom_call" | custom-call | tf_op jit(solution)/shard_map/deliver/pallas_call | solution.py:312

commit v6 on v5

--- a/solution.py
+++ b/solution.py
@@ -36,7 +36,12 @@
 def invert(A, between):
     lane = lax.broadcasted_iota(jnp.int32, (8, R), 1)
     sub = lax.broadcasted_iota(jnp.int32, (8, R), 0)
-    A = list(A)
+    t = [jnp.where(lane == sub + 8 * m, A[m], 0.0) for m in range(16)]
+    down = [lax.rsqrt(jnp.sum(d, axis=1, keepdims=True)) for d in t]
+    while len(t) > 1:
+        t = [t[q] + t[q + 1] for q in range(0, len(t), 2)]
+    across = lax.rsqrt(jnp.sum(t[0], axis=0, keepdims=True))
+    A = [A[m] * across * down[m] for m in range(16)]
     for p in range(R // 16):
         between(p)
         l0 = 16 * p
@@ -51,16 +56,16 @@
             a, b = sub_bcast(c[i][v], s), sub_bcast(c[i + 1][v], s)
             d, e = sub_bcast(c[i][v], s + 1), sub_bcast(c[i + 1][v], s + 1)
             det = 1.0 / (a * e - b * d)
-            g0 = [(c[i][u] * e - c[i + 1][u] * d) * det for u in range(2)]
-            g1 = [(c[i + 1][u] * a - c[i][u] * b) * det for u in range(2)]
-            g0[v] = jnp.where(sub == s, -(e * det), jnp.where(sub == s + 1, d * det, g0[v]))
-            g1[v] = jnp.where(sub == s, b * det, jnp.where(sub == s + 1, -(a * det), g1[v]))
+            g0 = [c[i][u] * e - c[i + 1][u] * d for u in range(2)]
+            g1 = [c[i + 1][u] * a - c[i][u] * b for u in range(2)]
+            g0[v] = jnp.where(sub == s, -e, jnp.where(sub == s + 1, d, g0[v]))
+            g1[v] = jnp.where(sub == s, b, jnp.where(sub == s + 1, -a, g1[v]))
             hit = (sub == s) | (sub == s + 1)
 
             def step(t):
                 r0, r1 = sub_bcast(t[v], s), sub_bcast(t[v], s + 1)
                 kept = [jnp.where(hit, 0.0, t[u]) if u == v else t[u] for u in range(2)]
-                return [kept[u] - (g0[u] * r0 + g1[u] * r1) for u in range(2)]
+                return [kept[u] - (g0[u] * r0 + g1[u] * r1) * det for u in range(2)]
 
             for m in range(i + 2, 16):
                 c[m] = step(c[m])
@@ -78,7 +83,7 @@
                 new[m] = jnp.where(inside, 0.0, A[m]) - update[8 * m : 8 * m + 8]
         new[own[0]], new[own[1]] = rows
         A = new
-    return A
+    return [A[m] * across * down[m] for m in range(16)]
 
 
 def kernel(

time: 34.5 us -> 34.4 us (level)
  no operation moved by 1% of the time
where the time goes in v6:
time: 34.4 us; the launch traced here: 34.2 us
  Pallas kernels  33.6 us (98%)
  between operations  0.64 us (2%)
    pallas_call x1, Pallas kernels, shards(): pl.pallas_call(kernel, out_shape=(pltpu.VMEM((64, R), F32), pltpu.VMEM((R...  32.9 us

profile of v6, /device:TPU:1, one launch (start us, length us, event | category | flops | bytes accessed | tf_op | source)
XLA Modules:
  0.0 34.2 jit_solution(6811223693663763367)
XLA Ops:
  0.6 32.9 %update.1 = (f32[64,128]{1,0:T(8,128)S(1)}, f32[128,128]{1,0:T(8,128)S(1)}) custom-call(f32[64,128]{1,0:T(8,128)} %base.1, bf16[64,256,128]{2,1,0:T(8,128)(2,1)} %opb.1, bf16[64,256,128]{2,1,0:T(8,128)(2,1)} %opc.1, bf16[16,256]{1,0:T(8,128)(2,1)} %bitcast.6, bf16[16,256]{1,0:T(8,128)(2,1)} %bitcast.7, f32[16,256]{1,0:T(8,128)} %bitcast.4, f32[16,256]{1,0:T(8,128)} %bitcast.5), custom_call_target="tpu_custom_call" | custom-call | tf_op jit(solution)/shard_map/update/pallas_call | solution.py:285
  33.6 0.7 %deliver.1 = (f32[64,128]{1,0:T(8,128)}, f32[128,128]{1,0:T(8,128)}) custom-call(f32[64,128]{1,0:T(8,128)S(1)} %get-tuple-element.4.fa, f32[128,128]{1,0:T(8,128)S(1)} %get-tuple-element.5.gn), custom_call_target="tpu_custom_call" | custom-call | tf_op jit(solution)/shard_map/deliver/pallas_call | solution.py:317

commit v7 on v6

--- a/solution.py
+++ b/solution.py
@@ -49,7 +49,6 @@
         own = [2 * p, 2 * p + 1]
         ahead = [m for m in (2 * p + 2, 2 * p + 3) if m < 16]
         c = [[lane_bcast(A[u], l0 + i) for u in own] for i in range(16)]
-        early = {m: [lane_bcast(A[m], l0 + i) for i in range(16)] for m in ahead}
         rows = [jnp.where(inside, jnp.where(lane - l0 == sub + 8 * k, 1.0, 0.0), A[u]) for k, u in enumerate(own)]
         for i in range(0, 16, 2):
             v, s = i // 8, i % 8
@@ -72,7 +71,7 @@
             rows = step(rows)
         new = list(A)
         for m in ahead:
-            t = [early[m][i] * sub_bcast(rows[i // 8], i % 8) for i in range(16)]
+            t = [lane_bcast(A[m], l0 + i) * sub_bcast(rows[i // 8], i % 8) for i in range(16)]
             while len(t) > 1:
                 t = [t[q] + t[q + 1] for q in range(0, len(t), 2)]
             new[m] = jnp.where(inside, 0.0, A[m]) - t[0]
@@ -257,9 +256,10 @@
     mtm = mtm_v[0] + mtm_v[1]
     inverse = inv[...]
     own = ag_m[x].reshape(64, R)
-    fa_out[...] = jnp.dot(own, inverse, precision=HIGH, preferred_element_type=F32)
-    half = jnp.dot(mtm, inverse, precision=HIGH, preferred_element_type=F32)
-    gram_a = lax.dot_general(inverse, half, (((0,), (0,)), ((), ())), precision=HIGH, preferred_element_type=F32)
+    both = jnp.dot(jnp.concatenate([mtm, own], axis=0), inverse, precision=HIGH, preferred_element_type=F32)
+    half = both[:R]
+    fa_out[...] = both[R:]
+    gram_a = jnp.dot(inverse, half, precision=HIGH, preferred_element_type=F32)
     gn_out[...] = gram_a / ROWS * gram_c
 
     for copy in send_am + [swap, over_g]:

time: 34.4 us -> 34.4 us (level)
  no operation moved by 1% of the time
where the time goes in v7:
time: 34.4 us; the launch traced here: 34.2 us
  Pallas kernels  33.6 us (98%)
  between operations  0.64 us (2%)
    pallas_call x1, Pallas kernels, shards(): pl.pallas_call(kernel, out_shape=(pltpu.VMEM((64, R), F32), pltpu.VMEM((R...  32.9 us

profile of v7, /device:TPU:1, one launch (start us, length us, event | category | flops | bytes accessed | tf_op | source)
XLA Modules:
  0.0 34.2 jit_solution(10358508457671376124)
XLA Ops:
  0.6 32.9 %update.1 = (f32[64,128]{1,0:T(8,128)S(1)}, f32[128,128]{1,0:T(8,128)S(1)}) custom-call(f32[64,128]{1,0:T(8,128)} %base.1, bf16[64,256,128]{2,1,0:T(8,128)(2,1)} %opb.1, bf16[64,256,128]{2,1,0:T(8,128)(2,1)} %opc.1, bf16[16,256]{1,0:T(8,128)(2,1)} %bitcast.6, bf16[16,256]{1,0:T(8,128)(2,1)} %bitcast.7, f32[16,256]{1,0:T(8,128)} %bitcast.4, f32[16,256]{1,0:T(8,128)} %bitcast.5), custom_call_target="tpu_custom_call" | custom-call | tf_op jit(solution)/shard_map/update/pallas_call | solution.py:285
  33.6 0.7 %deliver.1 = (f32[64,128]{1,0:T(8,128)}, f32[128,128]{1,0:T(8,128)}) custom-call(f32[64,128]{1,0:T(8,128)S(1)} %get-tuple-element.4.fa, f32[128,128]{1,0:T(8,128)S(1)} %get-tuple-element.5.gn), custom_call_target="tpu_custom_call" | custom-call | tf_op jit(solution)/shard_map/deliver/pallas_call | solution.py:317

commit v8 on v7

--- a/solution.py
+++ b/solution.py
@@ -119,7 +119,7 @@
         pl.semaphore_signal(barrier, inc=1, device_id=(at_row(dx, dcore), at_col(dz, dy)), device_id_type=MESH)
     for copy in small:
         copy.start()
-    for copy in small:
+    for copy in small[:4]:
         copy.wait()
     rv_f[x, core] = st_f[core]
     pass_f[x] = st_f[1 - core]
@@ -217,6 +217,7 @@
     for copy in send_zm:
         copy.wait_recv()
     summed = ((z_m[0] + z_m[1]) + (z_m[2] + z_m[3])) + ((z_m[4] + z_m[5]) + (z_m[6] + z_m[7]))
+    small[4].wait()
     ag_m[x, y] = base_v[pl.ds(pl.multiple_of(16 * y, 16), 16), :] + summed
     send_am = []
     for k, (dx, dy) in enumerate(SAME_CORE):

time: 34.4 us -> 34.4 us (level)
  no operation moved by 1% of the time
where the time goes in v8:
time: 34.4 us; the launch traced here: 34.3 us
  Pallas kernels  33.6 us (98%)
  between operations  0.64 us (2%)
    pallas_call x1, Pallas kernels, shards(): pl.pallas_call(kernel, out_shape=(pltpu.VMEM((64, R), F32), pltpu.VMEM((R...  33 us

profile of v8, /device:TPU:1, one launch (start us, length us, event | category | flops | bytes accessed | tf_op | source)
XLA Modules:
  0.0 34.3 jit_solution(4543325649312233485)
XLA Ops:
  0.6 33.0 %update.1 = (f32[64,128]{1,0:T(8,128)S(1)}, f32[128,128]{1,0:T(8,128)S(1)}) custom-call(f32[64,128]{1,0:T(8,128)} %base.1, bf16[64,256,128]{2,1,0:T(8,128)(2,1)} %opb.1, bf16[64,256,128]{2,1,0:T(8,128)(2,1)} %opc.1, bf16[16,256]{1,0:T(8,128)(2,1)} %bitcast.6, bf16[16,256]{1,0:T(8,128)(2,1)} %bitcast.7, f32[16,256]{1,0:T(8,128)} %bitcast.4, f32[16,256]{1,0:T(8,128)} %bitcast.5), custom_call_target="tpu_custom_call" | custom-call | tf_op jit(solution)/shard_map/update/pallas_call | solution.py:286
  33.6 0.7 %deliver.1 = (f32[64,128]{1,0:T(8,128)}, f32[128,128]{1,0:T(8,128)}) custom-call(f32[64,128]{1,0:T(8,128)S(1)} %get-tuple-element.4.fa, f32[128,128]{1,0:T(8,128)S(1)} %get-tuple-element.5.gn), custom_call_target="tpu_custom_call" | custom-call | tf_op jit(solution)/shard_map/deliver/pallas_call | solution.py:318
